TPU v7x, 128 devices: a whole 4x4x4 slice. The times are simulated.
128 devices in a mesh: site: 2 (over core), sector: 64 (over z, x, y).
Axes of the slice: x: 4, y: 4, z: 4, core: 2. Of those that a mesh axis runs over, the one named last changes fastest.
Arguments:
- environment: bfloat16 [256, 128, 30, 128], P('sector'), may hold values from -6 to 6
- amplitudes: bfloat16 [2, 256, 4, 128, 128], P('site', 'sector'), may hold values from -0.5 to 0.5
- mpo_weight: bfloat16 [2, 30, 4, 4, 30], P('site'), may hold values from -0.75 to 0.75
- mpo_mask: int32 [2, 30, 30], P('site'), may hold values 0 or 1
- sector_count: int32 [64], replicated, may hold values from 1 to 4, as said below
Outputs:
- env_out: bfloat16 [2, 256, 128, 30, 128], P('site', 'sector')
Inputs may be any that keep to these rules, and one draw needn't show every extreme that they name: `sector_count`: every owner holds one or more sectors and some owner holds 4; owner 64 - 2 holds exactly one sector.
All inputs are finite; a program needn't handle non-finite values. No bound on the sum of `mpo_mask` on one device may be relied on, other than what follows from the above.
Results may differ from a plain program's by a relative error of at most 0.017.
Values may be sent and summed in bfloat16 or wider, within the bound.
No kernel may reach another device: no remote copies, remote signals or barrier semaphores. Data moves between devices by JAX's collectives and lax.ppermute only.
A program may use at most 128 MiB of HBM per device.

v0:
```python
import functools

import jax
import jax.numpy as jnp
from jax import lax
from jax.experimental import pallas as pl
from jax.experimental.pallas import tpu as pltpu
from jax.sharding import PartitionSpec as P

S = 128
W = 30
HALF = 15
CUTS = ((0, 8), (8, HALF))
Q_FLOPS = 8_000_000_000
OPEN = 0
N_CUT = len(CUTS)
AXES = ("site", "sector")
F32 = jnp.float32
BF16 = jnp.bfloat16
MIB = 1024 * 1024
HBM = pl.BlockSpec(memory_space=pltpu.HBM)
VMEM = pl.BlockSpec(memory_space=pltpu.VMEM)
ANY = pl.BlockSpec(memory_space=pl.ANY)


def iota(shape, dim):
    return lax.broadcasted_iota(jnp.int32, shape, dim)


def place(sizes):
    owner = lax.axis_index("sector")
    return sizes[owner], lax.axis_index("site"), owner


def expand_operator(core, site, states, w_own, w_oth, wk):
    row_v = iota((8 * HALF, W), 0) // 8 + core * HALF
    pick_v = (row_v == iota((8 * HALF, W), 1)).astype(BF16)
    spot = iota((W, 8 * W), 1) // 8
    if site:
        spot = jnp.where(core == 0, spot, jnp.where(spot < HALF, spot + HALF, spot - HALF))
    pick_w = (spot == iota((W, 8 * W), 0)).astype(BF16)
    diagonal = (iota((8 * HALF, 8 * W), 0) % 8) == (iota((8 * HALF, 8 * W), 1) % 8)

    def block(s, s2):
        chosen = jnp.where(core == site, w_own[s, s2].astype(F32), w_oth[s, s2].astype(F32)).astype(BF16)
        rows = lax.dot_general(pick_v, chosen, (((1,), (1,)), ((), ())), preferred_element_type=F32).astype(BF16)
        full = jnp.dot(rows, pick_w, preferred_element_type=F32)
        return jnp.where(diagonal, full, 0.0).astype(BF16)

    if 0 in states:
        wk[0, : 8 * HALF, : 8 * W] = block(0, 0)
    if 3 in states:
        wk[1, : 8 * HALF, : 8 * W] = block(3, 3)
    if 1 in states:
        upper = jnp.concatenate([block(1, 1), block(1, 2)], axis=1)
        lower = jnp.concatenate([block(2, 1), block(2, 2)], axis=1)
        wk[2] = jnp.concatenate([upper, lower], axis=0)


def first_steps(left, amps, states, wk, z):
    columns = jnp.concatenate([amps[s] for s in states], axis=1) if len(states) > 1 else amps[states[0]]
    rights = []
    for g in range(8):
        block = left[:, 16 * g : 16 * g + 16, :].reshape(W * 16, S)
        c = jnp.dot(block, columns, preferred_element_type=F32)
        c = c.reshape(W, 16, S * len(states))
        low = c[:, :8, :].reshape(W * 8, S * len(states)).astype(BF16)
        high = c[:, 8:, :].reshape(W * 8, S * len(states)).astype(BF16)
        rights.append(
            {
                s: jnp.concatenate([low[:, S * k : S * k + S], high[:, S * k : S * k + S]], axis=1)
                for k, s in enumerate(states)
            }
        )

    def keep(s, g, total):
        total = total.reshape(HALF, 8, 2 * S)
        z[s, :, 16 * g : 16 * g + 16, :] = jnp.concatenate([total[:, :, :S], total[:, :, S:]], axis=1).astype(BF16)

    for g in range(8):
        for s, p in ((0, 0), (3, 1)):
            if s in states:
                keep(s, g, jnp.dot(wk[p, : 8 * HALF, : 8 * W], rights[g][s], preferred_element_type=F32))
        if 1 in states:
            both = jnp.concatenate([rights[g][1], rights[g][2]], axis=0)
            total = jnp.dot(wk[2], both, preferred_element_type=F32)
            keep(1, g, total[: 8 * HALF])
            keep(2, g, total[8 * HALF :])


def last_step(amps, states, z, sink):
    turned = [amps[s].astype(F32).T.astype(BF16) for s in states]
    lhs = jnp.concatenate(turned, axis=1) if len(states) > 1 else turned[0]

    def right(v):
        return jnp.concatenate([z[s, v] for s in states], axis=0) if len(states) > 1 else z[states[0], v]

    for v in range(0, HALF, 2):
        count = min(2, HALF - v)
        rhs = jnp.concatenate([right(v), right(v + 1)], axis=1) if count > 1 else right(v)
        out = jnp.dot(lhs, rhs, preferred_element_type=F32)
        for i in range(count):
            sink(v + i, out[:, S * i : S * i + S])


def form_left(slot, left, refs):
    @pl.when(slot == 0)
    def _():
        for half in range(2):
            for (a, b), ref in zip(CUTS, refs[0][half]):
                left[half * HALF + a : half * HALF + b] = ref[...]

    for k in (1, 2, 3):
        @pl.when(slot == k)
        def _(k=k):
            for half in range(2):
                left[half * HALF : half * HALF + HALF] = refs[k][half][...]


def grouped(refs):
    rest = refs[2 * N_CUT :]
    return ((refs[:N_CUT], refs[N_CUT : 2 * N_CUT]), *((rest[k], rest[3 + k]) for k in range(3)))


def pick_amp(core, site, amp_refs, slot, s):
    if site:
        return amp_refs[0][slot, s]
    return jnp.where(core == site, amp_refs[0][slot, s].astype(F32), amp_refs[1][slot, s].astype(F32)).astype(BF16)


def y_kernel(site, sizes, lefts, amp_refs, w_own, w_oth, outs, left, wk, z):
    count, core, _ = place(sizes)
    slot = count - 1
    expand_operator(core, site, (3,), w_own, w_oth, wk)
    amps = {3: pick_amp(core, site, amp_refs, slot, 3)}
    if site:
        form_left(slot, left, grouped(lefts))
    first_steps(left if site else lefts[0], amps, (3,), wk, z)

    def sink(v, block):
        for (a, b), out in zip(CUTS, outs):
            if a <= v < b:
                out[v - a] = block.astype(BF16)

    last_step(amps, (3,), z, sink)


def x_kernel(site, sizes, lefts, amp_refs, w_own, w_oth, outs, left, wk, z, acc, *sems):
    count, core, _ = place(sizes)
    prior = jnp.maximum(count - 2, 0)
    if site == 0:
        fetch = pltpu.make_async_copy(lefts[1].at[prior], left, sems[0])
        fetch.start()
    expand_operator(core, site, (1, 2, 3), w_own, w_oth, wk)
    if site:
        form_left(count - 1, left, grouped(lefts))
    amps = {s: pick_amp(core, site, amp_refs, count - 1, s) for s in (1, 2)}
    first_steps(left if site else lefts[0], amps, (1, 2), wk, z)

    def put(read):
        def sink(v, block):
            for (a, b), out in zip(CUTS, outs):
                if a <= v < b:
                    out[v - a] = read(v, block).astype(BF16)

        return sink

    def keep(v, block):
        acc[v] = block

    last_step(amps, (1, 2), z, keep)
    if site == 0:
        fetch.wait()

    @pl.when(count >= 2)
    def _():
        if site:
            form_left(prior, left, grouped(lefts))
        amps = {3: pick_amp(core, site, amp_refs, prior, 3)}
        first_steps(left, amps, (3,), wk, z)
        last_step(amps, (3,), z, put(lambda v, block: acc[v] + block))

    @pl.when(count < 2)
    def _():
        for (a, b), out in zip(CUTS, outs):
            out[...] = acc[a:b].astype(BF16)


def q_kernel(site, sizes, lefts, amp_refs, w_own, w_oth, outs, left, wk, z, next_one, next_two, *sems):
    out = outs[0]
    lefts, y_refs = lefts[:-N_CUT], lefts[-N_CUT:]
    count, core, owner = place(sizes)
    step = pl.program_id(0)

    def fetch(slot):
        return pltpu.make_async_copy(lefts[0].at[slot], left.at[slot % 2], sems[0].at[slot % 2])

    @pl.when(step == 0)
    def _():
        if site == 0:
            fetch(0).start()
        else:
            pl.when(core == 0)(lambda: start_all(known_blocks(lefts, outs[1], sems[0])))
        expand_operator(core, site, (0, 1, 2, 3), w_own, w_oth, wk)
        next_one[...] = jnp.zeros_like(next_one)
        next_two[...] = jnp.zeros_like(next_two)

    if site == 0:
        @pl.when(step + 1 < count)
        def _():
            fetch(step + 1).start()

        for s in range(4):
            later_amp = jnp.where(core == 1, amp_refs[0][step, s].astype(F32), amp_refs[1][step, s].astype(F32))
            outs[1][step, s] = later_amp.astype(BF16)

        @pl.when(step < count)
        def _():
            fetch(step).wait()

        source = left.at[step % 2]
    else:
        @pl.when(step < count)
        def _():
            form_left(step, left, grouped(lefts))

        source = left

    @pl.when(jnp.logical_and(step == 1, owner > 0))
    def _():
        for (a, b), ref in zip(CUTS, y_refs):
            next_one[a:b] = next_one[a:b] + ref[...].astype(F32)

    def sink_zero(v, block):
        out[step, v] = (block + next_one[v]).astype(BF16)

    def sink_one(v, block):
        next_one[v] = block + next_two[v]

    def sink_two(v, block):
        next_two[v] = block

    def work(states):
        amps = {s: pick_amp(core, site, amp_refs, step, s) for s in states}
        first_steps(source, amps, states, wk, z)
        last_step(amps, (0,), z, sink_zero)
        if 1 in states:
            last_step(amps, (1, 2), z, sink_one)
        if 3 in states:
            last_step(amps, (3,), z, sink_two)

    @pl.when(step < count - 2)
    def _():
        work((0, 3, 1, 2))

    @pl.when(jnp.logical_and(step == count - 2, step >= 0))
    def _():
        work((0, 1, 2))

    @pl.when(step == count - 1)
    def _():
        work((0,))

    @pl.when(step >= count)
    def _():
        out[step] = jnp.zeros((HALF, S, S), BF16)

    if site:
        def own_half():
            return [pltpu.make_async_copy(out.at[k], outs[1].at[k, HALF:], sems[0].at[k - 1]) for k in (1, 2, 3)]

        @pl.when(step == 3)
        def _():
            pl.when(core == 0)(lambda: wait_all(known_blocks(lefts, outs[1], sems[0])))

            @pl.when(core == 1)
            def _():
                start_all(own_half())
                wait_all(own_half())


def start_all(copies):
    for copy in copies:
        copy.start()


def wait_all(copies):
    for copy in copies:
        copy.wait()


def known_blocks(lefts, out, sems):
    copies = []

    def add(ref, slot, v, length):
        copies.append(pltpu.make_async_copy(ref, out.at[slot, v : v + length], sems.at[len(copies)]))

    blocks = grouped(lefts)
    for half in range(2):
        for (a, b), ref in zip(CUTS, blocks[0][half]):
            add(ref, 0, half * HALF + a, b - a)
        for slot in (1, 2, 3):
            add(blocks[slot][half], slot, half * HALF, HALF)
    return copies


CUT_SHAPES = [(b - a, S, S) for a, b in CUTS]


def call(kernel, site, grid, left_specs, shapes, scratch, flops, sizes, lefts, amps, ops, after=(), out_specs=None):
    n_left, n_out, n_after, n_amp = len(lefts), len(shapes), len(after), len(amps)

    def body(sizes, *refs):
        left_refs, refs = refs[:n_left], refs[n_left:]
        amp_refs, op_refs, refs = refs[:n_amp], refs[n_amp : n_amp + 2], refs[n_amp + 2 + n_after :]
        kernel(site, sizes, left_refs, amp_refs, *op_refs, refs[:n_out], *refs[n_out:])

    return pl.pallas_call(
        body,
        grid_spec=pltpu.PrefetchScalarGridSpec(
            num_scalar_prefetch=1,
            grid=(grid,),
            in_specs=left_specs + [VMEM] * (n_amp + 2) + [ANY] * n_after,
            out_specs=out_specs or [VMEM] * n_out,
            scratch_shapes=scratch,
        ),
        out_shape=[jax.ShapeDtypeStruct(shape, BF16) for shape in shapes],
        cost_estimate=pl.CostEstimate(flops=flops, bytes_accessed=4_000_000, transcendentals=0),
        compiler_params=pltpu.CompilerParams(vmem_limit_bytes=(46 if kernel is q_kernel and site == 0 else 24) * MIB, dimension_semantics=("arbitrary",)),
        name=kernel.__name__ + str(site),
    )(sizes, *lefts, *amps, *ops, *after)


def work_space():
    return [pltpu.VMEM((3, 16 * HALF, 16 * W), BF16), pltpu.VMEM((4, HALF, S, S), BF16)]


def edge_two(site, sizes, lefts, amps, ops):
    left = pltpu.VMEM((W, S, S) if site else (1, 8, S), BF16)
    return call(
        y_kernel, site, 1, [VMEM] * len(lefts), CUT_SHAPES, [left] + work_space(), 2_000_000_000, sizes, lefts, amps, ops
    )


def edge_one(site, sizes, lefts, amps, ops, after):
    scratch = [pltpu.VMEM((W, S, S), BF16)] + work_space() + [pltpu.VMEM((HALF, S, S), F32)]
    specs = [VMEM] * len(lefts)
    if site == 0:
        scratch.append(pltpu.SemaphoreType.DMA)
        specs = [VMEM, HBM]
    return call(x_kernel, site, 1, specs, CUT_SHAPES, scratch, 4_000_000_000, sizes, lefts, amps, ops, after)


def inner(site, sizes, lefts, amps, ops, after):
    left = pltpu.VMEM((W, S, S) if site else (2, W, S, S), BF16)
    scratch = [left] + work_space() + [pltpu.VMEM((HALF, S, S), F32)] * 2
    specs, shapes = [VMEM] * len(lefts), [(4, HALF, S, S), (4, W, S, S) if site else (4, 4, S, S)]
    scratch.append(pltpu.SemaphoreType.DMA((2 * N_CUT + 6 if site else 2,)))
    if site == 0:
        specs = [HBM] + [VMEM] * N_CUT
    out_specs = [VMEM, HBM if site else VMEM]
    return call(q_kernel, site, 4, specs, shapes, scratch, Q_FLOPS, sizes, lefts, amps, ops, after, out_specs)


def fetch_last(sizes, env):
    def body(sizes, env, out, sem):
        copy = pltpu.make_async_copy(env.at[place(sizes)[0] - 1], out, sem)
        copy.start()
        copy.wait()

    return pl.pallas_call(
        body,
        in_specs=[pl.BlockSpec(memory_space=pltpu.SMEM), HBM],
        out_specs=VMEM,
        scratch_shapes=[pltpu.SemaphoreType.DMA],
        out_shape=jax.ShapeDtypeStruct((W, S, S), BF16),
        compiler_params=pltpu.CompilerParams(vmem_limit_bytes=52 * MIB),
        name="fetch_last",
    )(sizes, env)


def finish(written, zero, zero_oth, rest_oth):
    def body(written, *refs):
        own, other, rest = refs[:N_CUT], refs[N_CUT : 2 * N_CUT], refs[2 * N_CUT : 2 * N_CUT + 3]
        out, sems = refs[2 * N_CUT + 3 :]

        @pl.when(lax.axis_index("site") == 1)
        def _():
            copies = []

            def add(ref, slot, v, length):
                copies.append(pltpu.make_async_copy(ref, out.at[slot, v : v + length], sems.at[len(copies)]))

            for k in range(3):
                add(rest[k], k + 1, 0, HALF)
            for half, parts in enumerate((other, own)):
                for (a, b), ref in zip(CUTS, parts):
                    add(ref, 0, half * HALF + a, b - a)
            start_all(copies)
            wait_all(copies)

    return pl.pallas_call(
        body,
        in_specs=[HBM] + [VMEM] * (2 * N_CUT + 3),
        out_specs=HBM,
        scratch_shapes=[pltpu.SemaphoreType.DMA((2 * N_CUT + 3,))],
        out_shape=jax.ShapeDtypeStruct((4, W, S, S), BF16),
        input_output_aliases={0: 0},
        compiler_params=pltpu.CompilerParams(vmem_limit_bytes=4 * MIB),
        name="finish",
    )(written, *zero, *zero_oth, *rest_oth)


def operator_blocks(weight, mask):
    kept = jnp.where(mask[:, None, None, :] != 0, weight, jnp.zeros_like(weight))
    return jnp.transpose(kept, (1, 2, 0, 3))


def later(x, *others):
    return lax.optimization_barrier((x, *others))[0]


def plus(x, y, take):
    return (x.astype(F32) + jnp.where(take, y.astype(F32), 0.0)).astype(BF16)


def shards(owners, environment, amplitudes, mpo_weight, mpo_mask, sector_count):
    owner = lax.axis_index("sector")
    across = [(c * owners + o, (1 - c) * owners + o) for c in range(2) for o in range(owners)]
    ahead = [(c * owners + o, c * owners + (o + 1) % owners) for c in range(2) for o in range(owners)]

    def swap(x):
        return lax.ppermute(x, AXES, across)

    def onward(x):
        return lax.ppermute(x, AXES, ahead)

    def final_onward(x):
        return lax.ppermute(x, AXES, [pair for pair in ahead if pair[1] % owners > 0])

    env = jnp.transpose(environment, (0, 2, 1, 3))
    own_ops = operator_blocks(mpo_weight[0], mpo_mask[0])
    amps = (amplitudes[0], swap(amplitudes[0]))
    ops = (own_ops, swap(own_ops))

    env_last = fetch_last(sector_count, env)
    edge_left, back_left, lefts = (env_last,), (env_last, env), (env,)
    inward = owner > 0
    for site in range(2):
        y_out = edge_two(site, sector_count, edge_left, amps, ops)
        y_in = [(final_onward if k == OPEN else onward)(y) for k, y in enumerate(y_out)]
        if site == 0:
            count = lax.dynamic_index_in_dim(later(sector_count, y_out[0]), owner, 0, keepdims=False)
            pass_on = jnp.logical_and(count == 1, inward)
        x_out = edge_one(site, sector_count, back_left, amps, ops, y_out)
        x_sent = [plus(x, y, pass_on) for x, y in zip(x_out, y_in)]
        x_in = [(final_onward if k == OPEN else onward)(x) for k, x in enumerate(x_sent)]
        made = inner(site, sector_count, (*lefts, *y_in), amps, ops, x_sent)
        inside = made[0]
        rest = [inside[k] for k in (1, 2, 3)]
        rest_oth = [swap(later(part, y_in[-1])) for part in rest]
        zero = [plus(later(inside, x)[0, a:b], x, inward) for (a, b), x in zip(CUTS, x_in)]
        if site == 0:
            zero_oth = [swap(block) for block in zero]
            lefts = edge_left = back_left = (*zero, *zero_oth, *rest, *rest_oth)
            amps = (made[1],)
        else:
            zero_oth = [swap(block) for block in zero]
            result = finish(made[1], zero, zero_oth, rest_oth)
    return jnp.transpose(result, (0, 2, 1, 3))[None]


def solution(mesh):
    placed = (
        P("sector", None, None, None),
        P("site", "sector", None, None, None),
        P("site", None, None, None, None),
        P("site", None, None),
        P(),
    )
    return jax.shard_map(
        functools.partial(shards, mesh.shape["sector"]),
        mesh=mesh,
        in_specs=placed,
        out_specs=P("site", "sector", None, None, None),
        check_vma=False,
    )
```

profile of v0, /device:TPU:33, one launch (start us, length us, event | category | flops | bytes accessed | tf_op | source)
XLA Modules:
  0.0 77.9 jit_solution(10265315250308977421)
XLA Ops:
  3.1 1.8 %fetch_last.1.refs_0_ = bf16[30,128,128]{2,1,0:T(8,128)(2,1)S(1)} custom-call(s32[64]{0:T(128)S(1)} %copy-done.1, bf16[4,30,128,128]{3,2,1,0:T(8,128)(2,1)} %bitcast.39), custom_call_target="tpu_custom_call" | custom-call | tf_op jit(solution)/shard_map/fetch_last/pallas_call | solution.py:371
  4.9 2.2 %y_kernel0.1 = (bf16[8,128,128]{2,1,0:T(8,128)(2,1)S(1)}, bf16[7,128,128]{2,1,0:T(8,128)(2,1)}) custom-call(s32[64]{0:T(128)S(1)} %copy-done.1, bf16[30,128,128]{2,1,0:T(8,128)(2,1)S(1)} %fetch_last.1.refs_0_, bf16[4,4,128,128]{3,2,1,0:T(8,128)(2,1)S(1)} %bitcast.43, bf16[4,4,128,128]{3,2,1,0:T(8,128)(2,1)S(1)} %collective-permute-done.refs_2_.refs_3_.refs_4_, ...), custom_call_target="tpu_custom_call" | custom-call | flops 2000000000 | bytes 4000000 | tf_op jit(solution)/shard_map/y_kernel0/pallas_call | solution.py:318
  7.1 1.3 %collective-permute-start.3 = (bf16[7,128,128]{2,1,0:T(8,128)(2,1)}, bf16[7,128,128]{2,1,0:T(8,128)(2,1)S(1)}, u32[]{:S(2)}, u32[]{:S(2)}) collective-permute-start(bf16[7,128,128]{2,1,0:T(8,128)(2,1)} %get-tuple-element.29.refs_7_), channel_id=1, source_target_pairs={{0,1},{1,2},{2,3},{3,4},{4,5},{5,6},{6,7},{7,8},{8,9},{9,10},{10,1... | collective-permute-start | bytes 688136 | tf_op jit(solution)/shard_map/ppermute | solution.py:436
  8.4 3.2 %collective-permute-start.2 = (bf16[8,128,128]{2,1,0:T(8,128)(2,1)S(1)}, bf16[8,128,128]{2,1,0:T(8,128)(2,1)S(1)}, u32[]{:S(2)}, u32[]{:S(2)}) collective-permute-start(bf16[8,128,128]{2,1,0:T(8,128)(2,1)S(1)} %get-tuple-element.28.refs_6_), channel_id=1, source_target_pairs={{0,1},{1,2},{2,3},{3,4},{4,5},{5,6},{6,7},{7,8},{8,9},{9,10},{10,1... | collective-permute-start | bytes 786440 | tf_op jit(solution)/shard_map/ppermute | solution.py:439
  11.6 3.5 %x_kernel0.1 = (bf16[8,128,128]{2,1,0:T(8,128)(2,1)S(1)}, bf16[7,128,128]{2,1,0:T(8,128)(2,1)S(1)}) custom-call(s32[64]{0:T(128)S(1)} %copy-done.2, bf16[30,128,128]{2,1,0:T(8,128)(2,1)S(1)} %fetch_last.1.refs_0_, bf16[4,30,128,128]{3,2,1,0:T(8,128)(2,1)S(1)} %bitcast.41, bf16[4,4,128,128]{3,2,1,0:T(8,128)(2,1)S(1)} %bitcast.44, ...), custom_call_target="tpu_custom_call" | custom-call | flops 4000000000 | bytes 4000000 | tf_op jit(solution)/shard_map/x_kernel0/pallas_call | solution.py:318
  16.5 1.7 %collective-permute-done.3.refs_2_ = bf16[7,128,128]{2,1,0:T(8,128)(2,1)S(1)} collective-permute-done((bf16[7,128,128]{2,1,0:T(8,128)(2,1)}, bf16[7,128,128]{2,1,0:T(8,128)(2,1)S(1)}, u32[]{:S(2)}, u32[]{:S(2)}) %collective-permute-start.3) | collective-permute-done | bytes 229408 | tf_op jit(solution)/shard_map/ppermute | solution.py:436
  18.4 5.5 %collective-permute-done.2.refs_1_ = bf16[8,128,128]{2,1,0:T(8,128)(2,1)S(1)} collective-permute-done((bf16[8,128,128]{2,1,0:T(8,128)(2,1)S(1)}, bf16[8,128,128]{2,1,0:T(8,128)(2,1)S(1)}, u32[]{:S(2)}, u32[]{:S(2)}) %collective-permute-start.2) | collective-permute-done | bytes 262176 | tf_op jit(solution)/shard_map/ppermute | solution.py:439
  24.0 1.9 %collective-permute-start.4 = (bf16[8,128,128]{2,1,0:T(8,128)(2,1)S(1)}, bf16[8,128,128]{2,1,0:T(8,128)(2,1)S(1)}, u32[]{:S(2)}, u32[]{:S(2)}) collective-permute-start(bf16[8,128,128]{2,1,0:T(8,128)(2,1)S(1)} %add_convert_fusion.1.refs_7_), channel_id=1, source_target_pairs={{0,1},{1,2},{2,3},{3,4},{4,5},{5,6},{6,7},{7,8},{8,9},{9,10},{10,1... | collective-permute-start | bytes 786440 | tf_op jit(solution)/shard_map/ppermute | solution.py:439
  25.9 5.0 %q_kernel0.1 = (bf16[4,15,128,128]{3,2,1,0:T(8,128)(2,1)S(1)}, bf16[4,4,128,128]{3,2,1,0:T(8,128)(2,1)S(1)}) custom-call(s32[64]{0:T(128)S(1)} %copy-done.2, bf16[4,30,128,128]{3,2,1,0:T(8,128)(2,1)} %bitcast.40, bf16[8,128,128]{2,1,0:T(8,128)(2,1)S(1)} %collective-permute-done.2.refs_1_, bf16[7,128,128]{2,1,0:T(8,128)(2,1)S(1)} %collective-permute-done.3.refs_2_, ...), custom_call_target="tpu_custom_call" | custom-call | flops 8000000000 | bytes 4000000 | tf_op jit(solution)/shard_map/q_kernel0/pallas_call | solution.py:318
  31.0 1.4 %collective-permute-start.10 = (bf16[15,128,128]{2,1,0:T(8,128)(2,1)S(1)}, bf16[15,128,128]{2,1,0:T(8,128)(2,1)S(1)}, u32[]{:S(2)}, u32[]{:S(2)}) collective-permute-start(bf16[15,128,128]{2,1,0:T(8,128)(2,1)S(1)} %get-tuple-element.38.refs_6_), channel_id=1, source_target_pairs={{0,64},{1,65},{2,66},{3,67},{4,68},{5,69},{6,70},{7,71},{8,72},{9,... | collective-permute-start | bytes 1474568 | tf_op jit(solution)/shard_map/ppermute | solution.py:433
  32.9 3.6 %collective-permute-done.4 = bf16[8,128,128]{2,1,0:T(8,128)(2,1)S(1)} collective-permute-done((bf16[8,128,128]{2,1,0:T(8,128)(2,1)S(1)}, bf16[8,128,128]{2,1,0:T(8,128)(2,1)S(1)}, u32[]{:S(2)}, u32[]{:S(2)}) %collective-permute-start.4) | collective-permute-done | bytes 262176 | tf_op jit(solution)/shard_map/ppermute | solution.py:439
  36.6 2.3 %collective-permute-start.6 = (bf16[8,128,128]{2,1,0:T(8,128)(2,1)S(1)}, bf16[8,128,128]{2,1,0:T(8,128)(2,1)S(1)}, u32[]{:S(2)}, u32[]{:S(2)}) collective-permute-start(bf16[8,128,128]{2,1,0:T(8,128)(2,1)S(1)} %fusion.1.refs_0_), channel_id=1, source_target_pairs={{0,64},{1,65},{2,66},{3,67},{4,68},{5,69},{6,70},{7,71},{8,72},{9,... | collective-permute-start | bytes 786440 | tf_op jit(solution)/shard_map/ppermute | solution.py:433
  39.3 1.5 %collective-permute-done.7.refs_3_ = bf16[7,128,128]{2,1,0:T(8,128)(2,1)S(1)} collective-permute-done((bf16[7,128,128]{2,1,0:T(8,128)(2,1)S(1)}, bf16[7,128,128]{2,1,0:T(8,128)(2,1)S(1)}, u32[]{:S(2)}, u32[]{:S(2)}) %collective-permute-start.7) | collective-permute-done | bytes 229408 | tf_op jit(solution)/shard_map/ppermute | solution.py:433
  40.8 1.7 %y_kernel1.1 = (bf16[8,128,128]{2,1,0:T(8,128)(2,1)S(1)}, bf16[7,128,128]{2,1,0:T(8,128)(2,1)S(1)}) custom-call(s32[64]{0:T(128)S(1)} %copy-done.2, bf16[8,128,128]{2,1,0:T(8,128)(2,1)S(1)} %fusion.1.refs_0_, bf16[7,128,128]{2,1,0:T(8,128)(2,1)S(1)} %fusion.3.refs_1_, bf16[8,128,128]{2,1,0:T(8,128)(2,1)S(1)} %collective-permute-done.6.refs_2_, ...), custom_call_target="tpu_custom_call" | custom-call | flops 2000000000 | bytes 4000000 | tf_op jit(solution)/shard_map/y_kernel1/pallas_call | solution.py:318
  42.6 1.9 %collective-permute-start.11 = (bf16[8,128,128]{2,1,0:T(8,128)(2,1)S(1)}, bf16[8,128,128]{2,1,0:T(8,128)(2,1)S(1)}, u32[]{:S(2)}, u32[]{:S(2)}) collective-permute-start(bf16[8,128,128]{2,1,0:T(8,128)(2,1)S(1)} %get-tuple-element.40.refs_13_), channel_id=1, source_target_pairs={{0,1},{1,2},{2,3},{3,4},{4,5},{5,6},{6,7},{7,8},{8,9},{9,10},{10,1... | collective-permute-start | bytes 786440 | tf_op jit(solution)/shard_map/ppermute | solution.py:439
  44.5 3.5 %x_kernel1.1 = (bf16[8,128,128]{2,1,0:T(8,128)(2,1)S(1)}, bf16[7,128,128]{2,1,0:T(8,128)(2,1)S(1)}) custom-call(s32[64]{0:T(128)S(1)} %copy-done.2, bf16[8,128,128]{2,1,0:T(8,128)(2,1)S(1)} %fusion.1.refs_0_, bf16[7,128,128]{2,1,0:T(8,128)(2,1)S(1)} %fusion.3.refs_1_, bf16[8,128,128]{2,1,0:T(8,128)(2,1)S(1)} %collective-permute-done.6.refs_2_, ...), custom_call_target="tpu_custom_call" | custom-call | flops 4000000000 | bytes 4000000 | tf_op jit(solution)/shard_map/x_kernel1/pallas_call | solution.py:318
  48.0 5.8 %collective-permute-done.12.refs_11_ = bf16[7,128,128]{2,1,0:T(8,128)(2,1)S(1)} collective-permute-done((bf16[7,128,128]{2,1,0:T(8,128)(2,1)S(1)}, bf16[7,128,128]{2,1,0:T(8,128)(2,1)S(1)}, u32[]{:S(2)}, u32[]{:S(2)}) %collective-permute-start.12) | collective-permute-done | bytes 229408 | tf_op jit(solution)/shard_map/ppermute | solution.py:436
  54.0 5.5 %collective-permute-done.11.refs_10_ = bf16[8,128,128]{2,1,0:T(8,128)(2,1)S(1)} collective-permute-done((bf16[8,128,128]{2,1,0:T(8,128)(2,1)S(1)}, bf16[8,128,128]{2,1,0:T(8,128)(2,1)S(1)}, u32[]{:S(2)}, u32[]{:S(2)}) %collective-permute-start.11) | collective-permute-done | bytes 262176 | tf_op jit(solution)/shard_map/ppermute | solution.py:439
  59.6 1.9 %collective-permute-start.13 = (bf16[8,128,128]{2,1,0:T(8,128)(2,1)S(1)}, bf16[8,128,128]{2,1,0:T(8,128)(2,1)S(1)}, u32[]{:S(2)}, u32[]{:S(2)}) collective-permute-start(bf16[8,128,128]{2,1,0:T(8,128)(2,1)S(1)} %add_convert_fusion.refs_15_), channel_id=1, source_target_pairs={{0,1},{1,2},{2,3},{3,4},{4,5},{5,6},{6,7},{7,8},{8,9},{9,10},{10,1... | collective-permute-start | bytes 786440 | tf_op jit(solution)/shard_map/ppermute | solution.py:439
  61.5 6.0 %q_kernel1.1 = (bf16[4,15,128,128]{3,2,1,0:T(8,128)(2,1)S(1)}, bf16[4,30,128,128]{3,2,1,0:T(8,128)(2,1)}) custom-call(s32[64]{0:T(128)S(1)} %copy-done.2, bf16[8,128,128]{2,1,0:T(8,128)(2,1)S(1)} %fusion.1.refs_0_, bf16[7,128,128]{2,1,0:T(8,128)(2,1)S(1)} %fusion.3.refs_1_, bf16[8,128,128]{2,1,0:T(8,128)(2,1)S(1)} %collective-permute-done.6.refs_2_, ...), custom_call_target="tpu_custom_call" | custom-call | flops 8000000000 | bytes 4000000 | tf_op jit(solution)/shard_map/q_kernel1/pallas_call | solution.py:318
  68.3 4.2 %collective-permute-done.13 = bf16[8,128,128]{2,1,0:T(8,128)(2,1)S(1)} collective-permute-done((bf16[8,128,128]{2,1,0:T(8,128)(2,1)S(1)}, bf16[8,128,128]{2,1,0:T(8,128)(2,1)S(1)}, u32[]{:S(2)}, u32[]{:S(2)}) %collective-permute-start.13) | collective-permute-done | bytes 262176 | tf_op jit(solution)/shard_map/ppermute | solution.py:439
  72.7 1.9 %collective-permute-start.15 = (bf16[8,128,128]{2,1,0:T(8,128)(2,1)S(1)}, bf16[8,128,128]{2,1,0:T(8,128)(2,1)S(1)}, u32[]{:S(2)}, u32[]{:S(2)}) collective-permute-start(bf16[8,128,128]{2,1,0:T(8,128)(2,1)S(1)} %fusion.refs_0_), channel_id=1, source_target_pairs={{0,64},{1,65},{2,66},{3,67},{4,68},{5,69},{6,70},{7,71},{8,72},{9,... | collective-permute-start | bytes 786440 | tf_op jit(solution)/shard_map/ppermute | solution.py:433
  74.8 1.5 %collective-permute-done.16.refs_3_ = bf16[7,128,128]{2,1,0:T(8,128)(2,1)S(1)} collective-permute-done((bf16[7,128,128]{2,1,0:T(8,128)(2,1)S(1)}, bf16[7,128,128]{2,1,0:T(8,128)(2,1)S(1)}, u32[]{:S(2)}, u32[]{:S(2)}) %collective-permute-start.16) | collective-permute-done | bytes 229408 | tf_op jit(solution)/shard_map/ppermute | solution.py:433
  76.3 1.5 %finish.1 = bf16[4,30,128,128]{3,2,1,0:T(8,128)(2,1)} custom-call(bf16[4,30,128,128]{3,2,1,0:T(8,128)(2,1)} %get-tuple-element.44.written, bf16[8,128,128]{2,1,0:T(8,128)(2,1)S(1)} %fusion.refs_0_, bf16[7,128,128]{2,1,0:T(8,128)(2,1)S(1)} %fusion.2.refs_1_, bf16[8,128,128]{2,1,0:T(8,128)(2,1)S(1)} %collective-permute-done.15.refs_2_, ...), custom_call_target="tpu_custom_call", output_to_operand_aliasing={{}: (0, {})} | custom-call | tf_op jit(solution)/shard_map/finish/pallas_call | solution.py:402
  (46 shorter events, 6.6 us)
Async XLA Ops:
  0.0 4.9 %collective-permute-start = (bf16[4,4,128,128]{3,2,1,0:T(8,128)(2,1)}, bf16[4,4,128,128]{3,2,1,0:T(8,128)(2,1)S(1)}, u32[]{:S(2)}, u32[]{:S(2)}) collective-permute-start(bf16[4,4,128,128]{3,2,1,0:T(8,128)(2,1)} %bitcast.42), channel_id=1, source_target_pairs={{0,64},{1,65},{2,66},{3,67},{4,68},{5,69},{6,70},{7,71},{8,72},{9,... | collective-permute-start | bytes 1572872 | tf_op jit(solution)/shard_map/ppermute | solution.py:433
  2.4 2.6 %collective-permute-start.1 = (bf16[4,4,30,30]{3,2,1,0:T(8,128)(2,1)S(1)}, bf16[4,4,30,30]{3,2,1,0:T(8,128)(2,1)S(1)}, u32[]{:S(2)}, u32[]{:S(2)}) collective-permute-start(bf16[4,4,30,30]{3,2,1,0:T(8,128)(2,1)S(1)} %fusion.4.refs_3_.refs_4_.refs_5_.refs_11_.refs_13_), channel_id=1, source_target_pairs={{0,64},{1,65},{2,66},{3,67},{4,68},{5,69},{6,70},{7,71},{8,72},{9,... | collective-permute-start | bytes 86408 | tf_op jit(solution)/shard_map/ppermute | solution.py:433
  2.5 0.7 copy-start.1
  3.1 1.8 %copy-start.3 = (bf16[1,4,4,128,128]{4,3,2,1,0:T(8,128)(2,1)S(1)}, bf16[1,4,4,128,128]{4,3,2,1,0:T(8,128)(2,1)}, u32[]{:S(2)}) copy-start(bf16[1,4,4,128,128]{4,3,2,1,0:T(8,128)(2,1)} %param.6) | copy-start | bytes 1572868
  4.9 6.7 %copy-start = (bf16[4,128,30,128]{3,1,2,0:T(8,128)(2,1)S(1)}, bf16[4,128,30,128]{3,1,2,0:T(8,128)(2,1)}, u32[]{:S(2)}) copy-start(bf16[4,128,30,128]{3,1,2,0:T(8,128)(2,1)} %param.5) | copy-start | bytes 11796484
  4.9 6.7 %copy-start.2 = (s32[64]{0:T(128)S(1)}, s32[64]{0:T(128)}, u32[]{:S(2)}) copy-start(s32[64]{0:T(128)} %sizes.13) | copy-start | bytes 772
  7.1 11.1 %collective-permute-start.3 = (bf16[7,128,128]{2,1,0:T(8,128)(2,1)}, bf16[7,128,128]{2,1,0:T(8,128)(2,1)S(1)}, u32[]{:S(2)}, u32[]{:S(2)}) collective-permute-start(bf16[7,128,128]{2,1,0:T(8,128)(2,1)} %get-tuple-element.29.refs_7_), channel_id=1, source_target_pairs={{0,1},{1,2},{2,3},{3,4},{4,5},{5,6},{6,7},{7,8},{8,9},{9,10},{10,1... | collective-permute-start | bytes 688136 | tf_op jit(solution)/shard_map/ppermute | solution.py:436
  8.4 15.4 %collective-permute-start.2 = (bf16[8,128,128]{2,1,0:T(8,128)(2,1)S(1)}, bf16[8,128,128]{2,1,0:T(8,128)(2,1)S(1)}, u32[]{:S(2)}, u32[]{:S(2)}) collective-permute-start(bf16[8,128,128]{2,1,0:T(8,128)(2,1)S(1)} %get-tuple-element.28.refs_6_), channel_id=1, source_target_pairs={{0,1},{1,2},{2,3},{3,4},{4,5},{5,6},{6,7},{7,8},{8,9},{9,10},{10,1... | collective-permute-start | bytes 786440 | tf_op jit(solution)/shard_map/ppermute | solution.py:439
  18.3 14.6 %collective-permute-start.5 = (bf16[7,128,128]{2,1,0:T(8,128)(2,1)S(1)}, bf16[7,128,128]{2,1,0:T(8,128)(2,1)S(1)}, u32[]{:S(2)}, u32[]{:S(2)}) collective-permute-start(bf16[7,128,128]{2,1,0:T(8,128)(2,1)S(1)} %add_convert_fusion.3.refs_8_), channel_id=1, source_target_pairs={{0,1},{1,2},{2,3},{3,4},{4,5},{5,6},{6,7},{7,8},{8,9},{9,10},{10,1... | collective-permute-start | bytes 688136 | tf_op jit(solution)/shard_map/ppermute | solution.py:436
  24.0 12.6 %collective-permute-start.4 = (bf16[8,128,128]{2,1,0:T(8,128)(2,1)S(1)}, bf16[8,128,128]{2,1,0:T(8,128)(2,1)S(1)}, u32[]{:S(2)}, u32[]{:S(2)}) collective-permute-start(bf16[8,128,128]{2,1,0:T(8,128)(2,1)S(1)} %add_convert_fusion.1.refs_7_), channel_id=1, source_target_pairs={{0,1},{1,2},{2,3},{3,4},{4,5},{5,6},{6,7},{7,8},{8,9},{9,10},{10,1... | collective-permute-start | bytes 786440 | tf_op jit(solution)/shard_map/ppermute | solution.py:439
  31.0 9.8 %collective-permute-start.10 = (bf16[15,128,128]{2,1,0:T(8,128)(2,1)S(1)}, bf16[15,128,128]{2,1,0:T(8,128)(2,1)S(1)}, u32[]{:S(2)}, u32[]{:S(2)}) collective-permute-start(bf16[15,128,128]{2,1,0:T(8,128)(2,1)S(1)} %get-tuple-element.38.refs_6_), channel_id=1, source_target_pairs={{0,64},{1,65},{2,66},{3,67},{4,68},{5,69},{6,70},{7,71},{8,72},{9,... | collective-permute-start | bytes 1474568 | tf_op jit(solution)/shard_map/ppermute | solution.py:433
  32.4 8.4 %collective-permute-start.9 = (bf16[15,128,128]{2,1,0:T(8,128)(2,1)S(1)}, bf16[15,128,128]{2,1,0:T(8,128)(2,1)S(1)}, u32[]{:S(2)}, u32[]{:S(2)}) collective-permute-start(bf16[15,128,128]{2,1,0:T(8,128)(2,1)S(1)} %get-tuple-element.37.refs_5_), channel_id=1, source_target_pairs={{0,64},{1,65},{2,66},{3,67},{4,68},{5,69},{6,70},{7,71},{8,72},{9,... | collective-permute-start | bytes 1474568 | tf_op jit(solution)/shard_map/ppermute | solution.py:433
  32.5 8.3 %collective-permute-start.8 = (bf16[15,128,128]{2,1,0:T(8,128)(2,1)S(1)}, bf16[15,128,128]{2,1,0:T(8,128)(2,1)S(1)}, u32[]{:S(2)}, u32[]{:S(2)}) collective-permute-start(bf16[15,128,128]{2,1,0:T(8,128)(2,1)S(1)} %get-tuple-element.36.refs_4_), channel_id=1, source_target_pairs={{0,64},{1,65},{2,66},{3,67},{4,68},{5,69},{6,70},{7,71},{8,72},{9,... | collective-permute-start | bytes 1474568 | tf_op jit(solution)/shard_map/ppermute | solution.py:433
  36.6 4.2 %collective-permute-start.6 = (bf16[8,128,128]{2,1,0:T(8,128)(2,1)S(1)}, bf16[8,128,128]{2,1,0:T(8,128)(2,1)S(1)}, u32[]{:S(2)}, u32[]{:S(2)}) collective-permute-start(bf16[8,128,128]{2,1,0:T(8,128)(2,1)S(1)} %fusion.1.refs_0_), channel_id=1, source_target_pairs={{0,64},{1,65},{2,66},{3,67},{4,68},{5,69},{6,70},{7,71},{8,72},{9,... | collective-permute-start | bytes 786440 | tf_op jit(solution)/shard_map/ppermute | solution.py:433
  39.0 1.7 %collective-permute-start.7 = (bf16[7,128,128]{2,1,0:T(8,128)(2,1)S(1)}, bf16[7,128,128]{2,1,0:T(8,128)(2,1)S(1)}, u32[]{:S(2)}, u32[]{:S(2)}) collective-permute-start(bf16[7,128,128]{2,1,0:T(8,128)(2,1)S(1)} %fusion.3.refs_1_), channel_id=1, source_target_pairs={{0,64},{1,65},{2,66},{3,67},{4,68},{5,69},{6,70},{7,71},{8,72},{9,... | collective-permute-start | bytes 688136 | tf_op jit(solution)/shard_map/ppermute | solution.py:433
  42.5 11.4 %collective-permute-start.12 = (bf16[7,128,128]{2,1,0:T(8,128)(2,1)S(1)}, bf16[7,128,128]{2,1,0:T(8,128)(2,1)S(1)}, u32[]{:S(2)}, u32[]{:S(2)}) collective-permute-start(bf16[7,128,128]{2,1,0:T(8,128)(2,1)S(1)} %get-tuple-element.41.refs_14_), channel_id=1, source_target_pairs={{0,1},{1,2},{2,3},{3,4},{4,5},{5,6},{6,7},{7,8},{8,9},{9,10},{10,1... | collective-permute-start | bytes 688136 | tf_op jit(solution)/shard_map/ppermute | solution.py:436
  42.6 16.9 %collective-permute-start.11 = (bf16[8,128,128]{2,1,0:T(8,128)(2,1)S(1)}, bf16[8,128,128]{2,1,0:T(8,128)(2,1)S(1)}, u32[]{:S(2)}, u32[]{:S(2)}) collective-permute-start(bf16[8,128,128]{2,1,0:T(8,128)(2,1)S(1)} %get-tuple-element.40.refs_13_), channel_id=1, source_target_pairs={{0,1},{1,2},{2,3},{3,4},{4,5},{5,6},{6,7},{7,8},{8,9},{9,10},{10,1... | collective-permute-start | bytes 786440 | tf_op jit(solution)/shard_map/ppermute | solution.py:439
  54.0 14.4 %collective-permute-start.14 = (bf16[7,128,128]{2,1,0:T(8,128)(2,1)S(1)}, bf16[7,128,128]{2,1,0:T(8,128)(2,1)S(1)}, u32[]{:S(2)}, u32[]{:S(2)}) collective-permute-start(bf16[7,128,128]{2,1,0:T(8,128)(2,1)S(1)} %add_convert_fusion.2.refs_16_), channel_id=1, source_target_pairs={{0,1},{1,2},{2,3},{3,4},{4,5},{5,6},{6,7},{7,8},{8,9},{9,10},{10,1... | collective-permute-start | bytes 688136 | tf_op jit(solution)/shard_map/ppermute | solution.py:436
  59.6 13.0 %collective-permute-start.13 = (bf16[8,128,128]{2,1,0:T(8,128)(2,1)S(1)}, bf16[8,128,128]{2,1,0:T(8,128)(2,1)S(1)}, u32[]{:S(2)}, u32[]{:S(2)}) collective-permute-start(bf16[8,128,128]{2,1,0:T(8,128)(2,1)S(1)} %add_convert_fusion.refs_15_), channel_id=1, source_target_pairs={{0,1},{1,2},{2,3},{3,4},{4,5},{5,6},{6,7},{7,8},{8,9},{9,10},{10,1... | collective-permute-start | bytes 786440 | tf_op jit(solution)/shard_map/ppermute | solution.py:439
  67.6 8.6 %collective-permute-start.19 = (bf16[15,128,128]{2,1,0:T(8,128)(2,1)S(1)}, bf16[15,128,128]{2,1,0:T(8,128)(2,1)S(1)}, u32[]{:S(2)}, u32[]{:S(2)}) collective-permute-start(bf16[15,128,128]{2,1,0:T(8,128)(2,1)S(1)} %get-tuple-element.50), channel_id=1, source_target_pairs={{0,64},{1,65},{2,66},{3,67},{4,68},{5,69},{6,70},{7,71},{8,72},{9,... | collective-permute-start | bytes 1474568 | tf_op jit(solution)/shard_map/ppermute | solution.py:433
  67.7 8.5 %collective-permute-start.18 = (bf16[15,128,128]{2,1,0:T(8,128)(2,1)S(1)}, bf16[15,128,128]{2,1,0:T(8,128)(2,1)S(1)}, u32[]{:S(2)}, u32[]{:S(2)}) collective-permute-start(bf16[15,128,128]{2,1,0:T(8,128)(2,1)S(1)} %get-tuple-element.49), channel_id=1, source_target_pairs={{0,64},{1,65},{2,66},{3,67},{4,68},{5,69},{6,70},{7,71},{8,72},{9,... | collective-permute-start | bytes 1474568 | tf_op jit(solution)/shard_map/ppermute | solution.py:433
  68.2 8.0 %collective-permute-start.17 = (bf16[15,128,128]{2,1,0:T(8,128)(2,1)S(1)}, bf16[15,128,128]{2,1,0:T(8,128)(2,1)S(1)}, u32[]{:S(2)}, u32[]{:S(2)}) collective-permute-start(bf16[15,128,128]{2,1,0:T(8,128)(2,1)S(1)} %get-tuple-element.48), channel_id=1, source_target_pairs={{0,64},{1,65},{2,66},{3,67},{4,68},{5,69},{6,70},{7,71},{8,72},{9,... | collective-permute-start | bytes 1474568 | tf_op jit(solution)/shard_map/ppermute | solution.py:433
  72.7 3.6 %collective-permute-start.15 = (bf16[8,128,128]{2,1,0:T(8,128)(2,1)S(1)}, bf16[8,128,128]{2,1,0:T(8,128)(2,1)S(1)}, u32[]{:S(2)}, u32[]{:S(2)}) collective-permute-start(bf16[8,128,128]{2,1,0:T(8,128)(2,1)S(1)} %fusion.refs_0_), channel_id=1, source_target_pairs={{0,64},{1,65},{2,66},{3,67},{4,68},{5,69},{6,70},{7,71},{8,72},{9,... | collective-permute-start | bytes 786440 | tf_op jit(solution)/shard_map/ppermute | solution.py:433
  74.7 1.6 %collective-permute-start.16 = (bf16[7,128,128]{2,1,0:T(8,128)(2,1)S(1)}, bf16[7,128,128]{2,1,0:T(8,128)(2,1)S(1)}, u32[]{:S(2)}, u32[]{:S(2)}) collective-permute-start(bf16[7,128,128]{2,1,0:T(8,128)(2,1)S(1)} %fusion.2.refs_1_), channel_id=1, source_target_pairs={{0,64},{1,65},{2,66},{3,67},{4,68},{5,69},{6,70},{7,71},{8,72},{9,... | collective-permute-start | bytes 688136 | tf_op jit(solution)/shard_map/ppermute | solution.py:433
where the time goes:
time: 78.3 us; the launch traced here: 77.9 us
  waiting for transfers between devices  29.3 us (37%)
  Pallas kernels  25 us (32%)
  starting transfers between devices  18.5 us (24%)
  other arithmetic  2.34 us (3%)
  local copies, waits for them, and re-layouts  1.66 us (2%)
  between operations  1.15 us (1%)
    pallas_call x6, Pallas kernels, call(): pl.pallas_call(body, grid_spec=pltpu.PrefetchScalarGridSpec(num_scalar_pr...  21.8 us
    ppermute x4, waiting for transfers between devices, final_onward(): lax.ppermute(x, AXES, [pair for pair in ahead if pair[1] % owners > 0])  18.7 us
    ppermute x4, starting transfers between devices, final_onward(): lax.ppermute(x, AXES, [pair for pair in ahead if pair[1] % owners > 0])  8.96 us
    ppermute x12, starting transfers between devices, swap(): return lax.ppermute(x, AXES, across)  8 us
    ppermute x4, waiting for transfers between devices, onward(): return lax.ppermute(x, AXES, ahead)  7.59 us
    ppermute x12, waiting for transfers between devices, swap(): return lax.ppermute(x, AXES, across)  2.97 us
    pallas_call x1, Pallas kernels, fetch_last(): pl.pallas_call(body, in_specs=[pl.BlockSpec(memory_space=pltpu.SMEM), HBM...  1.76 us
  transfers between devices with their start and end apart: 20, of which 8 were waited for; matrix products, arithmetic and copies ran while one was open for 4% of the time, Pallas kernels for 25%

commit v1 on v0

--- a/solution.py
+++ b/solution.py
@@ -48,13 +48,13 @@
         return jnp.where(diagonal, full, 0.0).astype(BF16)
 
     if 0 in states:
-        wk[0, : 8 * HALF, : 8 * W] = block(0, 0)
+        wk[0][0] = block(0, 0)
     if 3 in states:
-        wk[1, : 8 * HALF, : 8 * W] = block(3, 3)
+        wk[0][1] = block(3, 3)
     if 1 in states:
         upper = jnp.concatenate([block(1, 1), block(1, 2)], axis=1)
         lower = jnp.concatenate([block(2, 1), block(2, 2)], axis=1)
-        wk[2] = jnp.concatenate([upper, lower], axis=0)
+        wk[1][...] = jnp.concatenate([upper, lower], axis=0)
 
 
 def first_steps(left, amps, states, wk, z):
@@ -80,10 +80,10 @@
     for g in range(8):
         for s, p in ((0, 0), (3, 1)):
             if s in states:
-                keep(s, g, jnp.dot(wk[p, : 8 * HALF, : 8 * W], rights[g][s], preferred_element_type=F32))
+                keep(s, g, jnp.dot(wk[0][p], rights[g][s], preferred_element_type=F32))
         if 1 in states:
             both = jnp.concatenate([rights[g][1], rights[g][2]], axis=0)
-            total = jnp.dot(wk[2], both, preferred_element_type=F32)
+            total = jnp.dot(wk[1][...], both, preferred_element_type=F32)
             keep(1, g, total[: 8 * HALF])
             keep(2, g, total[8 * HALF :])
 
@@ -313,7 +313,8 @@
     def body(sizes, *refs):
         left_refs, refs = refs[:n_left], refs[n_left:]
         amp_refs, op_refs, refs = refs[:n_amp], refs[n_amp : n_amp + 2], refs[n_amp + 2 + n_after :]
-        kernel(site, sizes, left_refs, amp_refs, *op_refs, refs[:n_out], *refs[n_out:])
+        left, wk_single, wk_pair, *others = refs[n_out:]
+        kernel(site, sizes, left_refs, amp_refs, *op_refs, refs[:n_out], left, (wk_single, wk_pair), *others)
 
     return pl.pallas_call(
         body,
@@ -332,7 +333,7 @@
 
 
 def work_space():
-    return [pltpu.VMEM((3, 16 * HALF, 16 * W), BF16), pltpu.VMEM((4, HALF, S, S), BF16)]
+    return [pltpu.VMEM((2, 8 * HALF, 8 * W), BF16), pltpu.VMEM((16 * HALF, 16 * W), BF16), pltpu.VMEM((4, HALF, S, S), BF16)]
 
 
 def edge_two(site, sizes, lefts, amps, ops):

time: 78.3 us -> 78.3 us (level)
  Pallas kernels: 25 us -> 19.7 us
  waiting for transfers between devices: 29.3 us -> 34.6 us
    pallas_call x6, Pallas kernels: 21.8 us -> 16.4 us  [call(): pl.pallas_call(body, grid_spec=pltpu.PrefetchScalarGridSpec(num_scalar_pr...]
    ppermute x4, waiting for transfers between devices: 18.7 us -> 22.5 us  [final_onward(): lax.ppermute(x, AXES, [pair for pair in ahead if pair[1] % owners > 0])]
    ppermute x4, waiting for transfers between devices: 7.59 us -> 9.18 us  [onward(): return lax.ppermute(x, AXES, ahead)]
  transfers between devices with their start and end apart: 20 -> 20, of which waited for: 8 -> 8; matrix products, arithmetic and copies ran while one was open for 4% -> 4% of each run, Pallas kernels for 25% -> 18%
where the time goes in v1:
time: 78.3 us; the launch traced here: 77.9 us
  waiting for transfers between devices  34.6 us (44%)
  Pallas kernels  19.7 us (25%)
  starting transfers between devices  18.5 us (24%)
  other arithmetic  2.34 us (3%)
  local copies, waits for them, and re-layouts  1.66 us (2%)
  between operations  1.15 us (1%)
    ppermute x4, waiting for transfers between devices, final_onward(): lax.ppermute(x, AXES, [pair for pair in ahead if pair[1] % owners > 0])  22.5 us
    pallas_call x6, Pallas kernels, call(): pl.pallas_call(body, grid_spec=pltpu.PrefetchScalarGridSpec(num_scalar_pr...  16.4 us
    ppermute x4, waiting for transfers between devices, onward(): return lax.ppermute(x, AXES, ahead)  9.18 us
    ppermute x4, starting transfers between devices, final_onward(): lax.ppermute(x, AXES, [pair for pair in ahead if pair[1] % owners > 0])  8.96 us
    ppermute x12, starting transfers between devices, swap(): return lax.ppermute(x, AXES, across)  8.01 us
    ppermute x12, waiting for transfers between devices, swap(): return lax.ppermute(x, AXES, across)  2.97 us
    pallas_call x1, Pallas kernels, fetch_last(): pl.pallas_call(body, in_specs=[pl.BlockSpec(memory_space=pltpu.SMEM), HBM...  1.76 us
  transfers between devices with their start and end apart: 20, of which 8 were waited for; matrix products, arithmetic and copies ran while one was open for 4% of the time, Pallas kernels for 18%

profile of v1, /device:TPU:33, one launch (start us, length us, event | category | flops | bytes accessed | tf_op | source)
XLA Modules:
  0.0 77.9 jit_solution(7528135348554775365)
XLA Ops:
  3.1 1.8 %fetch_last.1.refs_0_ = bf16[30,128,128]{2,1,0:T(8,128)(2,1)S(1)} custom-call(s32[64]{0:T(128)S(1)} %copy-done.1, bf16[4,30,128,128]{3,2,1,0:T(8,128)(2,1)} %bitcast.39), custom_call_target="tpu_custom_call" | custom-call | tf_op jit(solution)/shard_map/fetch_last/pallas_call | solution.py:372
  4.9 2.2 %y_kernel0.1 = (bf16[8,128,128]{2,1,0:T(8,128)(2,1)S(1)}, bf16[7,128,128]{2,1,0:T(8,128)(2,1)}) custom-call(s32[64]{0:T(128)S(1)} %copy-done.1, bf16[30,128,128]{2,1,0:T(8,128)(2,1)S(1)} %fetch_last.1.refs_0_, bf16[4,4,128,128]{3,2,1,0:T(8,128)(2,1)S(1)} %bitcast.43, bf16[4,4,128,128]{3,2,1,0:T(8,128)(2,1)S(1)} %collective-permute-done.refs_2_.refs_3_.refs_4_, ...), custom_call_target="tpu_custom_call" | custom-call | flops 2000000000 | bytes 4000000 | tf_op jit(solution)/shard_map/y_kernel0/pallas_call | solution.py:319
  7.1 1.3 %collective-permute-start.3 = (bf16[7,128,128]{2,1,0:T(8,128)(2,1)}, bf16[7,128,128]{2,1,0:T(8,128)(2,1)S(1)}, u32[]{:S(2)}, u32[]{:S(2)}) collective-permute-start(bf16[7,128,128]{2,1,0:T(8,128)(2,1)} %get-tuple-element.29.refs_7_), channel_id=1, source_target_pairs={{0,1},{1,2},{2,3},{3,4},{4,5},{5,6},{6,7},{7,8},{8,9},{9,10},{10,1... | collective-permute-start | bytes 688136 | tf_op jit(solution)/shard_map/ppermute | solution.py:437
  8.4 3.2 %collective-permute-start.2 = (bf16[8,128,128]{2,1,0:T(8,128)(2,1)S(1)}, bf16[8,128,128]{2,1,0:T(8,128)(2,1)S(1)}, u32[]{:S(2)}, u32[]{:S(2)}) collective-permute-start(bf16[8,128,128]{2,1,0:T(8,128)(2,1)S(1)} %get-tuple-element.28.refs_6_), channel_id=1, source_target_pairs={{0,1},{1,2},{2,3},{3,4},{4,5},{5,6},{6,7},{7,8},{8,9},{9,10},{10,1... | collective-permute-start | bytes 786440 | tf_op jit(solution)/shard_map/ppermute | solution.py:440
  11.6 2.7 %x_kernel0.1 = (bf16[8,128,128]{2,1,0:T(8,128)(2,1)S(1)}, bf16[7,128,128]{2,1,0:T(8,128)(2,1)S(1)}) custom-call(s32[64]{0:T(128)S(1)} %copy-done.2, bf16[30,128,128]{2,1,0:T(8,128)(2,1)S(1)} %fetch_last.1.refs_0_, bf16[4,30,128,128]{3,2,1,0:T(8,128)(2,1)S(1)} %bitcast.41, bf16[4,4,128,128]{3,2,1,0:T(8,128)(2,1)S(1)} %bitcast.44, ...), custom_call_target="tpu_custom_call" | custom-call | flops 4000000000 | bytes 4000000 | tf_op jit(solution)/shard_map/x_kernel0/pallas_call | solution.py:319
  15.7 2.5 %collective-permute-done.3.refs_2_ = bf16[7,128,128]{2,1,0:T(8,128)(2,1)S(1)} collective-permute-done((bf16[7,128,128]{2,1,0:T(8,128)(2,1)}, bf16[7,128,128]{2,1,0:T(8,128)(2,1)S(1)}, u32[]{:S(2)}, u32[]{:S(2)}) %collective-permute-start.3) | collective-permute-done | bytes 229408 | tf_op jit(solution)/shard_map/ppermute | solution.py:437
  18.4 5.5 %collective-permute-done.2.refs_1_ = bf16[8,128,128]{2,1,0:T(8,128)(2,1)S(1)} collective-permute-done((bf16[8,128,128]{2,1,0:T(8,128)(2,1)S(1)}, bf16[8,128,128]{2,1,0:T(8,128)(2,1)S(1)}, u32[]{:S(2)}, u32[]{:S(2)}) %collective-permute-start.2) | collective-permute-done | bytes 262176 | tf_op jit(solution)/shard_map/ppermute | solution.py:440
  24.0 1.9 %collective-permute-start.4 = (bf16[8,128,128]{2,1,0:T(8,128)(2,1)S(1)}, bf16[8,128,128]{2,1,0:T(8,128)(2,1)S(1)}, u32[]{:S(2)}, u32[]{:S(2)}) collective-permute-start(bf16[8,128,128]{2,1,0:T(8,128)(2,1)S(1)} %add_convert_fusion.1.refs_7_), channel_id=1, source_target_pairs={{0,1},{1,2},{2,3},{3,4},{4,5},{5,6},{6,7},{7,8},{8,9},{9,10},{10,1... | collective-permute-start | bytes 786440 | tf_op jit(solution)/shard_map/ppermute | solution.py:440
  25.9 3.1 %q_kernel0.1 = (bf16[4,15,128,128]{3,2,1,0:T(8,128)(2,1)S(1)}, bf16[4,4,128,128]{3,2,1,0:T(8,128)(2,1)S(1)}) custom-call(s32[64]{0:T(128)S(1)} %copy-done.2, bf16[4,30,128,128]{3,2,1,0:T(8,128)(2,1)} %bitcast.40, bf16[8,128,128]{2,1,0:T(8,128)(2,1)S(1)} %collective-permute-done.2.refs_1_, bf16[7,128,128]{2,1,0:T(8,128)(2,1)S(1)} %collective-permute-done.3.refs_2_, ...), custom_call_target="tpu_custom_call" | custom-call | flops 8000000000 | bytes 4000000 | tf_op jit(solution)/shard_map/q_kernel0/pallas_call | solution.py:319
  29.2 1.4 %collective-permute-start.10 = (bf16[15,128,128]{2,1,0:T(8,128)(2,1)S(1)}, bf16[15,128,128]{2,1,0:T(8,128)(2,1)S(1)}, u32[]{:S(2)}, u32[]{:S(2)}) collective-permute-start(bf16[15,128,128]{2,1,0:T(8,128)(2,1)S(1)} %get-tuple-element.38.refs_6_), channel_id=1, source_target_pairs={{0,64},{1,65},{2,66},{3,67},{4,68},{5,69},{6,70},{7,71},{8,72},{9,... | collective-permute-start | bytes 1474568 | tf_op jit(solution)/shard_map/ppermute | solution.py:434
  31.1 5.4 %collective-permute-done.4 = bf16[8,128,128]{2,1,0:T(8,128)(2,1)S(1)} collective-permute-done((bf16[8,128,128]{2,1,0:T(8,128)(2,1)S(1)}, bf16[8,128,128]{2,1,0:T(8,128)(2,1)S(1)}, u32[]{:S(2)}, u32[]{:S(2)}) %collective-permute-start.4) | collective-permute-done | bytes 262176 | tf_op jit(solution)/shard_map/ppermute | solution.py:440
  36.6 2.3 %collective-permute-start.6 = (bf16[8,128,128]{2,1,0:T(8,128)(2,1)S(1)}, bf16[8,128,128]{2,1,0:T(8,128)(2,1)S(1)}, u32[]{:S(2)}, u32[]{:S(2)}) collective-permute-start(bf16[8,128,128]{2,1,0:T(8,128)(2,1)S(1)} %fusion.1.refs_0_), channel_id=1, source_target_pairs={{0,64},{1,65},{2,66},{3,67},{4,68},{5,69},{6,70},{7,71},{8,72},{9,... | collective-permute-start | bytes 786440 | tf_op jit(solution)/shard_map/ppermute | solution.py:434
  39.3 1.5 %collective-permute-done.7.refs_3_ = bf16[7,128,128]{2,1,0:T(8,128)(2,1)S(1)} collective-permute-done((bf16[7,128,128]{2,1,0:T(8,128)(2,1)S(1)}, bf16[7,128,128]{2,1,0:T(8,128)(2,1)S(1)}, u32[]{:S(2)}, u32[]{:S(2)}) %collective-permute-start.7) | collective-permute-done | bytes 229408 | tf_op jit(solution)/shard_map/ppermute | solution.py:434
  40.8 1.7 %y_kernel1.1 = (bf16[8,128,128]{2,1,0:T(8,128)(2,1)S(1)}, bf16[7,128,128]{2,1,0:T(8,128)(2,1)S(1)}) custom-call(s32[64]{0:T(128)S(1)} %copy-done.2, bf16[8,128,128]{2,1,0:T(8,128)(2,1)S(1)} %fusion.1.refs_0_, bf16[7,128,128]{2,1,0:T(8,128)(2,1)S(1)} %fusion.3.refs_1_, bf16[8,128,128]{2,1,0:T(8,128)(2,1)S(1)} %collective-permute-done.6.refs_2_, ...), custom_call_target="tpu_custom_call" | custom-call | flops 2000000000 | bytes 4000000 | tf_op jit(solution)/shard_map/y_kernel1/pallas_call | solution.py:319
  42.6 1.9 %collective-permute-start.11 = (bf16[8,128,128]{2,1,0:T(8,128)(2,1)S(1)}, bf16[8,128,128]{2,1,0:T(8,128)(2,1)S(1)}, u32[]{:S(2)}, u32[]{:S(2)}) collective-permute-start(bf16[8,128,128]{2,1,0:T(8,128)(2,1)S(1)} %get-tuple-element.40.refs_13_), channel_id=1, source_target_pairs={{0,1},{1,2},{2,3},{3,4},{4,5},{5,6},{6,7},{7,8},{8,9},{9,10},{10,1... | collective-permute-start | bytes 786440 | tf_op jit(solution)/shard_map/ppermute | solution.py:440
  44.5 2.7 %x_kernel1.1 = (bf16[8,128,128]{2,1,0:T(8,128)(2,1)S(1)}, bf16[7,128,128]{2,1,0:T(8,128)(2,1)S(1)}) custom-call(s32[64]{0:T(128)S(1)} %copy-done.2, bf16[8,128,128]{2,1,0:T(8,128)(2,1)S(1)} %fusion.1.refs_0_, bf16[7,128,128]{2,1,0:T(8,128)(2,1)S(1)} %fusion.3.refs_1_, bf16[8,128,128]{2,1,0:T(8,128)(2,1)S(1)} %collective-permute-done.6.refs_2_, ...), custom_call_target="tpu_custom_call" | custom-call | flops 4000000000 | bytes 4000000 | tf_op jit(solution)/shard_map/x_kernel1/pallas_call | solution.py:319
  47.2 6.7 %collective-permute-done.12.refs_11_ = bf16[7,128,128]{2,1,0:T(8,128)(2,1)S(1)} collective-permute-done((bf16[7,128,128]{2,1,0:T(8,128)(2,1)S(1)}, bf16[7,128,128]{2,1,0:T(8,128)(2,1)S(1)}, u32[]{:S(2)}, u32[]{:S(2)}) %collective-permute-start.12) | collective-permute-done | bytes 229408 | tf_op jit(solution)/shard_map/ppermute | solution.py:437
  54.0 5.5 %collective-permute-done.11.refs_10_ = bf16[8,128,128]{2,1,0:T(8,128)(2,1)S(1)} collective-permute-done((bf16[8,128,128]{2,1,0:T(8,128)(2,1)S(1)}, bf16[8,128,128]{2,1,0:T(8,128)(2,1)S(1)}, u32[]{:S(2)}, u32[]{:S(2)}) %collective-permute-start.11) | collective-permute-done | bytes 262176 | tf_op jit(solution)/shard_map/ppermute | solution.py:440
  59.6 1.9 %collective-permute-start.13 = (bf16[8,128,128]{2,1,0:T(8,128)(2,1)S(1)}, bf16[8,128,128]{2,1,0:T(8,128)(2,1)S(1)}, u32[]{:S(2)}, u32[]{:S(2)}) collective-permute-start(bf16[8,128,128]{2,1,0:T(8,128)(2,1)S(1)} %add_convert_fusion.refs_15_), channel_id=1, source_target_pairs={{0,1},{1,2},{2,3},{3,4},{4,5},{5,6},{6,7},{7,8},{8,9},{9,10},{10,1... | collective-permute-start | bytes 786440 | tf_op jit(solution)/shard_map/ppermute | solution.py:440
  61.5 4.1 %q_kernel1.1 = (bf16[4,15,128,128]{3,2,1,0:T(8,128)(2,1)S(1)}, bf16[4,30,128,128]{3,2,1,0:T(8,128)(2,1)}) custom-call(s32[64]{0:T(128)S(1)} %copy-done.2, bf16[8,128,128]{2,1,0:T(8,128)(2,1)S(1)} %fusion.1.refs_0_, bf16[7,128,128]{2,1,0:T(8,128)(2,1)S(1)} %fusion.3.refs_1_, bf16[8,128,128]{2,1,0:T(8,128)(2,1)S(1)} %collective-permute-done.6.refs_2_, ...), custom_call_target="tpu_custom_call" | custom-call | flops 8000000000 | bytes 4000000 | tf_op jit(solution)/shard_map/q_kernel1/pallas_call | solution.py:319
  66.4 6.1 %collective-permute-done.13 = bf16[8,128,128]{2,1,0:T(8,128)(2,1)S(1)} collective-permute-done((bf16[8,128,128]{2,1,0:T(8,128)(2,1)S(1)}, bf16[8,128,128]{2,1,0:T(8,128)(2,1)S(1)}, u32[]{:S(2)}, u32[]{:S(2)}) %collective-permute-start.13) | collective-permute-done | bytes 262176 | tf_op jit(solution)/shard_map/ppermute | solution.py:440
  72.6 1.9 %collective-permute-start.15 = (bf16[8,128,128]{2,1,0:T(8,128)(2,1)S(1)}, bf16[8,128,128]{2,1,0:T(8,128)(2,1)S(1)}, u32[]{:S(2)}, u32[]{:S(2)}) collective-permute-start(bf16[8,128,128]{2,1,0:T(8,128)(2,1)S(1)} %fusion.refs_0_), channel_id=1, source_target_pairs={{0,64},{1,65},{2,66},{3,67},{4,68},{5,69},{6,70},{7,71},{8,72},{9,... | collective-permute-start | bytes 786440 | tf_op jit(solution)/shard_map/ppermute | solution.py:434
  74.8 1.5 %collective-permute-done.16.refs_3_ = bf16[7,128,128]{2,1,0:T(8,128)(2,1)S(1)} collective-permute-done((bf16[7,128,128]{2,1,0:T(8,128)(2,1)S(1)}, bf16[7,128,128]{2,1,0:T(8,128)(2,1)S(1)}, u32[]{:S(2)}, u32[]{:S(2)}) %collective-permute-start.16) | collective-permute-done | bytes 229408 | tf_op jit(solution)/shard_map/ppermute | solution.py:434
  76.3 1.5 %finish.1 = bf16[4,30,128,128]{3,2,1,0:T(8,128)(2,1)} custom-call(bf16[4,30,128,128]{3,2,1,0:T(8,128)(2,1)} %get-tuple-element.44.written, bf16[8,128,128]{2,1,0:T(8,128)(2,1)S(1)} %fusion.refs_0_, bf16[7,128,128]{2,1,0:T(8,128)(2,1)S(1)} %fusion.2.refs_1_, bf16[8,128,128]{2,1,0:T(8,128)(2,1)S(1)} %collective-permute-done.15.refs_2_, ...), custom_call_target="tpu_custom_call", output_to_operand_aliasing={{}: (0, {})} | custom-call | tf_op jit(solution)/shard_map/finish/pallas_call | solution.py:403
  (46 shorter events, 6.6 us)
Async XLA Ops:
  0.0 4.9 %collective-permute-start = (bf16[4,4,128,128]{3,2,1,0:T(8,128)(2,1)}, bf16[4,4,128,128]{3,2,1,0:T(8,128)(2,1)S(1)}, u32[]{:S(2)}, u32[]{:S(2)}) collective-permute-start(bf16[4,4,128,128]{3,2,1,0:T(8,128)(2,1)} %bitcast.42), channel_id=1, source_target_pairs={{0,64},{1,65},{2,66},{3,67},{4,68},{5,69},{6,70},{7,71},{8,72},{9,... | collective-permute-start | bytes 1572872 | tf_op jit(solution)/shard_map/ppermute | solution.py:434
  2.4 2.6 %collective-permute-start.1 = (bf16[4,4,30,30]{3,2,1,0:T(8,128)(2,1)S(1)}, bf16[4,4,30,30]{3,2,1,0:T(8,128)(2,1)S(1)}, u32[]{:S(2)}, u32[]{:S(2)}) collective-permute-start(bf16[4,4,30,30]{3,2,1,0:T(8,128)(2,1)S(1)} %fusion.4.refs_3_.refs_4_.refs_5_.refs_11_.refs_13_), channel_id=1, source_target_pairs={{0,64},{1,65},{2,66},{3,67},{4,68},{5,69},{6,70},{7,71},{8,72},{9,... | collective-permute-start | bytes 86408 | tf_op jit(solution)/shard_map/ppermute | solution.py:434
  2.5 0.7 copy-start.1
  3.1 1.8 %copy-start.3 = (bf16[1,4,4,128,128]{4,3,2,1,0:T(8,128)(2,1)S(1)}, bf16[1,4,4,128,128]{4,3,2,1,0:T(8,128)(2,1)}, u32[]{:S(2)}) copy-start(bf16[1,4,4,128,128]{4,3,2,1,0:T(8,128)(2,1)} %param.6) | copy-start | bytes 1572868
  4.9 6.7 %copy-start = (bf16[4,128,30,128]{3,1,2,0:T(8,128)(2,1)S(1)}, bf16[4,128,30,128]{3,1,2,0:T(8,128)(2,1)}, u32[]{:S(2)}) copy-start(bf16[4,128,30,128]{3,1,2,0:T(8,128)(2,1)} %param.5) | copy-start | bytes 11796484
  4.9 6.7 %copy-start.2 = (s32[64]{0:T(128)S(1)}, s32[64]{0:T(128)}, u32[]{:S(2)}) copy-start(s32[64]{0:T(128)} %sizes.13) | copy-start | bytes 772
  7.1 11.1 %collective-permute-start.3 = (bf16[7,128,128]{2,1,0:T(8,128)(2,1)}, bf16[7,128,128]{2,1,0:T(8,128)(2,1)S(1)}, u32[]{:S(2)}, u32[]{:S(2)}) collective-permute-start(bf16[7,128,128]{2,1,0:T(8,128)(2,1)} %get-tuple-element.29.refs_7_), channel_id=1, source_target_pairs={{0,1},{1,2},{2,3},{3,4},{4,5},{5,6},{6,7},{7,8},{8,9},{9,10},{10,1... | collective-permute-start | bytes 688136 | tf_op jit(solution)/shard_map/ppermute | solution.py:437
  8.4 15.4 %collective-permute-start.2 = (bf16[8,128,128]{2,1,0:T(8,128)(2,1)S(1)}, bf16[8,128,128]{2,1,0:T(8,128)(2,1)S(1)}, u32[]{:S(2)}, u32[]{:S(2)}) collective-permute-start(bf16[8,128,128]{2,1,0:T(8,128)(2,1)S(1)} %get-tuple-element.28.refs_6_), channel_id=1, source_target_pairs={{0,1},{1,2},{2,3},{3,4},{4,5},{5,6},{6,7},{7,8},{8,9},{9,10},{10,1... | collective-permute-start | bytes 786440 | tf_op jit(solution)/shard_map/ppermute | solution.py:440
  18.3 12.8 %collective-permute-start.5 = (bf16[7,128,128]{2,1,0:T(8,128)(2,1)S(1)}, bf16[7,128,128]{2,1,0:T(8,128)(2,1)S(1)}, u32[]{:S(2)}, u32[]{:S(2)}) collective-permute-start(bf16[7,128,128]{2,1,0:T(8,128)(2,1)S(1)} %add_convert_fusion.3.refs_8_), channel_id=1, source_target_pairs={{0,1},{1,2},{2,3},{3,4},{4,5},{5,6},{6,7},{7,8},{8,9},{9,10},{10,1... | collective-permute-start | bytes 688136 | tf_op jit(solution)/shard_map/ppermute | solution.py:437
  24.0 12.6 %collective-permute-start.4 = (bf16[8,128,128]{2,1,0:T(8,128)(2,1)S(1)}, bf16[8,128,128]{2,1,0:T(8,128)(2,1)S(1)}, u32[]{:S(2)}, u32[]{:S(2)}) collective-permute-start(bf16[8,128,128]{2,1,0:T(8,128)(2,1)S(1)} %add_convert_fusion.1.refs_7_), channel_id=1, source_target_pairs={{0,1},{1,2},{2,3},{3,4},{4,5},{5,6},{6,7},{7,8},{8,9},{9,10},{10,1... | collective-permute-start | bytes 786440 | tf_op jit(solution)/shard_map/ppermute | solution.py:440
  29.2 11.6 %collective-permute-start.10 = (bf16[15,128,128]{2,1,0:T(8,128)(2,1)S(1)}, bf16[15,128,128]{2,1,0:T(8,128)(2,1)S(1)}, u32[]{:S(2)}, u32[]{:S(2)}) collective-permute-start(bf16[15,128,128]{2,1,0:T(8,128)(2,1)S(1)} %get-tuple-element.38.refs_6_), channel_id=1, source_target_pairs={{0,64},{1,65},{2,66},{3,67},{4,68},{5,69},{6,70},{7,71},{8,72},{9,... | collective-permute-start | bytes 1474568 | tf_op jit(solution)/shard_map/ppermute | solution.py:434
  30.6 10.2 %collective-permute-start.9 = (bf16[15,128,128]{2,1,0:T(8,128)(2,1)S(1)}, bf16[15,128,128]{2,1,0:T(8,128)(2,1)S(1)}, u32[]{:S(2)}, u32[]{:S(2)}) collective-permute-start(bf16[15,128,128]{2,1,0:T(8,128)(2,1)S(1)} %get-tuple-element.37.refs_5_), channel_id=1, source_target_pairs={{0,64},{1,65},{2,66},{3,67},{4,68},{5,69},{6,70},{7,71},{8,72},{9,... | collective-permute-start | bytes 1474568 | tf_op jit(solution)/shard_map/ppermute | solution.py:434
  30.7 10.1 %collective-permute-start.8 = (bf16[15,128,128]{2,1,0:T(8,128)(2,1)S(1)}, bf16[15,128,128]{2,1,0:T(8,128)(2,1)S(1)}, u32[]{:S(2)}, u32[]{:S(2)}) collective-permute-start(bf16[15,128,128]{2,1,0:T(8,128)(2,1)S(1)} %get-tuple-element.36.refs_4_), channel_id=1, source_target_pairs={{0,64},{1,65},{2,66},{3,67},{4,68},{5,69},{6,70},{7,71},{8,72},{9,... | collective-permute-start | bytes 1474568 | tf_op jit(solution)/shard_map/ppermute | solution.py:434
  36.6 4.2 %collective-permute-start.6 = (bf16[8,128,128]{2,1,0:T(8,128)(2,1)S(1)}, bf16[8,128,128]{2,1,0:T(8,128)(2,1)S(1)}, u32[]{:S(2)}, u32[]{:S(2)}) collective-permute-start(bf16[8,128,128]{2,1,0:T(8,128)(2,1)S(1)} %fusion.1.refs_0_), channel_id=1, source_target_pairs={{0,64},{1,65},{2,66},{3,67},{4,68},{5,69},{6,70},{7,71},{8,72},{9,... | collective-permute-start | bytes 786440 | tf_op jit(solution)/shard_map/ppermute | solution.py:434
  39.0 1.7 %collective-permute-start.7 = (bf16[7,128,128]{2,1,0:T(8,128)(2,1)S(1)}, bf16[7,128,128]{2,1,0:T(8,128)(2,1)S(1)}, u32[]{:S(2)}, u32[]{:S(2)}) collective-permute-start(bf16[7,128,128]{2,1,0:T(8,128)(2,1)S(1)} %fusion.3.refs_1_), channel_id=1, source_target_pairs={{0,64},{1,65},{2,66},{3,67},{4,68},{5,69},{6,70},{7,71},{8,72},{9,... | collective-permute-start | bytes 688136 | tf_op jit(solution)/shard_map/ppermute | solution.py:434
  42.5 11.4 %collective-permute-start.12 = (bf16[7,128,128]{2,1,0:T(8,128)(2,1)S(1)}, bf16[7,128,128]{2,1,0:T(8,128)(2,1)S(1)}, u32[]{:S(2)}, u32[]{:S(2)}) collective-permute-start(bf16[7,128,128]{2,1,0:T(8,128)(2,1)S(1)} %get-tuple-element.41.refs_14_), channel_id=1, source_target_pairs={{0,1},{1,2},{2,3},{3,4},{4,5},{5,6},{6,7},{7,8},{8,9},{9,10},{10,1... | collective-permute-start | bytes 688136 | tf_op jit(solution)/shard_map/ppermute | solution.py:437
  42.6 16.9 %collective-permute-start.11 = (bf16[8,128,128]{2,1,0:T(8,128)(2,1)S(1)}, bf16[8,128,128]{2,1,0:T(8,128)(2,1)S(1)}, u32[]{:S(2)}, u32[]{:S(2)}) collective-permute-start(bf16[8,128,128]{2,1,0:T(8,128)(2,1)S(1)} %get-tuple-element.40.refs_13_), channel_id=1, source_target_pairs={{0,1},{1,2},{2,3},{3,4},{4,5},{5,6},{6,7},{7,8},{8,9},{9,10},{10,1... | collective-permute-start | bytes 786440 | tf_op jit(solution)/shard_map/ppermute | solution.py:440
  53.9 12.5 %collective-permute-start.14 = (bf16[7,128,128]{2,1,0:T(8,128)(2,1)S(1)}, bf16[7,128,128]{2,1,0:T(8,128)(2,1)S(1)}, u32[]{:S(2)}, u32[]{:S(2)}) collective-permute-start(bf16[7,128,128]{2,1,0:T(8,128)(2,1)S(1)} %add_convert_fusion.2.refs_16_), channel_id=1, source_target_pairs={{0,1},{1,2},{2,3},{3,4},{4,5},{5,6},{6,7},{7,8},{8,9},{9,10},{10,1... | collective-permute-start | bytes 688136 | tf_op jit(solution)/shard_map/ppermute | solution.py:437
  59.6 13.0 %collective-permute-start.13 = (bf16[8,128,128]{2,1,0:T(8,128)(2,1)S(1)}, bf16[8,128,128]{2,1,0:T(8,128)(2,1)S(1)}, u32[]{:S(2)}, u32[]{:S(2)}) collective-permute-start(bf16[8,128,128]{2,1,0:T(8,128)(2,1)S(1)} %add_convert_fusion.refs_15_), channel_id=1, source_target_pairs={{0,1},{1,2},{2,3},{3,4},{4,5},{5,6},{6,7},{7,8},{8,9},{9,10},{10,1... | collective-permute-start | bytes 786440 | tf_op jit(solution)/shard_map/ppermute | solution.py:440
  65.7 10.5 %collective-permute-start.19 = (bf16[15,128,128]{2,1,0:T(8,128)(2,1)S(1)}, bf16[15,128,128]{2,1,0:T(8,128)(2,1)S(1)}, u32[]{:S(2)}, u32[]{:S(2)}) collective-permute-start(bf16[15,128,128]{2,1,0:T(8,128)(2,1)S(1)} %get-tuple-element.50), channel_id=1, source_target_pairs={{0,64},{1,65},{2,66},{3,67},{4,68},{5,69},{6,70},{7,71},{8,72},{9,... | collective-permute-start | bytes 1474568 | tf_op jit(solution)/shard_map/ppermute | solution.py:434
  65.8 10.4 %collective-permute-start.18 = (bf16[15,128,128]{2,1,0:T(8,128)(2,1)S(1)}, bf16[15,128,128]{2,1,0:T(8,128)(2,1)S(1)}, u32[]{:S(2)}, u32[]{:S(2)}) collective-permute-start(bf16[15,128,128]{2,1,0:T(8,128)(2,1)S(1)} %get-tuple-element.49), channel_id=1, source_target_pairs={{0,64},{1,65},{2,66},{3,67},{4,68},{5,69},{6,70},{7,71},{8,72},{9,... | collective-permute-start | bytes 1474568 | tf_op jit(solution)/shard_map/ppermute | solution.py:434
  66.3 9.9 %collective-permute-start.17 = (bf16[15,128,128]{2,1,0:T(8,128)(2,1)S(1)}, bf16[15,128,128]{2,1,0:T(8,128)(2,1)S(1)}, u32[]{:S(2)}, u32[]{:S(2)}) collective-permute-start(bf16[15,128,128]{2,1,0:T(8,128)(2,1)S(1)} %get-tuple-element.48), channel_id=1, source_target_pairs={{0,64},{1,65},{2,66},{3,67},{4,68},{5,69},{6,70},{7,71},{8,72},{9,... | collective-permute-start | bytes 1474568 | tf_op jit(solution)/shard_map/ppermute | solution.py:434
  72.6 3.6 %collective-permute-start.15 = (bf16[8,128,128]{2,1,0:T(8,128)(2,1)S(1)}, bf16[8,128,128]{2,1,0:T(8,128)(2,1)S(1)}, u32[]{:S(2)}, u32[]{:S(2)}) collective-permute-start(bf16[8,128,128]{2,1,0:T(8,128)(2,1)S(1)} %fusion.refs_0_), channel_id=1, source_target_pairs={{0,64},{1,65},{2,66},{3,67},{4,68},{5,69},{6,70},{7,71},{8,72},{9,... | collective-permute-start | bytes 786440 | tf_op jit(solution)/shard_map/ppermute | solution.py:434
  74.7 1.6 %collective-permute-start.16 = (bf16[7,128,128]{2,1,0:T(8,128)(2,1)S(1)}, bf16[7,128,128]{2,1,0:T(8,128)(2,1)S(1)}, u32[]{:S(2)}, u32[]{:S(2)}) collective-permute-start(bf16[7,128,128]{2,1,0:T(8,128)(2,1)S(1)} %fusion.2.refs_1_), channel_id=1, source_target_pairs={{0,64},{1,65},{2,66},{3,67},{4,68},{5,69},{6,70},{7,71},{8,72},{9,... | collective-permute-start | bytes 688136 | tf_op jit(solution)/shard_map/ppermute | solution.py:434
